TPU v7x, 32 devices: a whole 2x2x4 slice. The times are simulated.
32 devices in a mesh: groups: 2 (over y), ctx: 4 (over x, core), shard: 4 (over z).
Axes of the slice: x: 2, y: 2, z: 4, core: 2. Of those that a mesh axis runs over, the one named last changes fastest.
Arguments:
- tokens: bfloat16 [2048, 8192], P(('groups', 'ctx'), 'shard'), parts along dimension 0, as said below
- gain: bfloat16 [8192], P('shard'), may hold values from 0.099609375 to 1.8984375
- w_query: bfloat16 [8192, 4096], P('ctx', 'shard'), may hold values from -0.0625 to 0.0625
- w_key: bfloat16 [1280, 4096], P('ctx', 'shard'), may hold values from -0.15625 to 0.15625
- w_value: bfloat16 [1280, 4096], P('ctx', 'shard'), may hold values from -0.15625 to 0.15625
- w_out: bfloat16 [4096, 8192], P('shard', 'ctx'), may hold values from -0.125 to 0.125
- latents: bfloat16 [2048, 1280], P(('groups', 'ctx')), parts along dimension 0, as said below
- image_pos: int32 [32], P(('groups', 'ctx')), parts along dimension 0, may hold values from -1 to 1023, as said below
- doc_lengths: int32 [12], P('groups'), parts along dimension 0, may hold values from 1 to 512, 1024 in all
- alpha: float32 [1], replicated, as said below
Outputs:
- mixed: bfloat16 [2048, 8192], P(('groups', 'ctx'), 'shard'), parts along dimension 0
There are 2 independent parts, one for each index of `groups`. A program takes and returns all parts, laid end to end along the dimension named above; an argument that names none is the same for every part. Nothing has to cross between parts.
Inputs may be any that keep to these rules, and one draw needn't show every extreme that they name: `image_pos`: slot c * 4 + k (k below 4) is either empty (-1) or holds a position from c * 256 + k * 64 to c * 256 + (k + 1) * 64 - 1; slot 0 is always empty and the last slot always holds position 1023; another slot is used with probability about 0.3, so runs of token blocks carry no image of their own. `latents`: entries lie within -170 to 170. `tokens`: entries lie within -22 to 22. `alpha`: the magnitude lies within 0.6 to 2.0, of either sign.
All inputs are finite; a program needn't handle non-finite values.
Results may differ from a plain program's by a relative error of at most 0.015.
Values may be sent and summed in bfloat16 or wider, within the bound.
A program may use at most 192 MiB of HBM per device.

v0:
```python
import jax
import jax.numpy as jnp
from jax import lax
from jax.sharding import PartitionSpec as P

HEAD_DIM = 128


def carried_in(value, axis, join, neutral):
    count, mine = (lax.axis_size(axis), lax.axis_index(axis))
    pieces = jax.tree.map(lambda part: lax.all_gather(part, axis), value)
    subtotal = jax.tree.map(
        lambda part, zero: jnp.full_like(part, 0) + jnp.asarray(zero, part.dtype), value, neutral
    )

    def lap(position, subtotal):
        longer = join(subtotal, jax.tree.map(lambda part: part[position], pieces))
        return jax.tree.map(lambda new, old: jnp.where(position < mine, new, old), longer, subtotal)

    return lax.fori_loop(0, count - 1, lap, subtotal)


def take_newer(before_part, after_part):
    newer_open = after_part[0] >= 0
    return tuple(
        (
            jnp.where(newer_open, after_item, before_item)
            for before_item, after_item in zip(before_part, after_part)
        )
    )


def body(tokens, gain, w_query, w_key, w_value, w_out, latents, image_pos, doc_lengths, alpha):
    tok_rows = tokens.shape[0]
    gathered, full_gain = (
        lax.all_gather(tokens, "shard", axis=1, tiled=True),
        lax.all_gather(gain, "shard", axis=0, tiled=True),
    )
    widened = gathered.astype(jnp.float32)
    mean_square = jnp.mean(widened * widened, axis=-1, keepdims=True)
    normed = (widened * lax.rsqrt(mean_square + 1e-06) * full_gain.astype(jnp.float32)).astype(
        jnp.bfloat16
    )
    key_panel, value_panel = (
        lax.all_gather(w_key, "ctx", axis=0, tiled=True),
        lax.all_gather(w_value, "ctx", axis=0, tiled=True),
    )
    query_panel, out_panel = (
        lax.all_gather(w_query, "ctx", axis=0, tiled=True),
        lax.all_gather(w_out, "ctx", axis=1, tiled=True),
    )
    queries = jnp.dot(normed, query_panel, preferred_element_type=jnp.float32).astype(jnp.bfloat16)
    slot_count = image_pos.shape[0]
    lat_rows = latents.shape[0] // slot_count
    slot_ids = jnp.arange(slot_count, dtype=jnp.int32)
    slot_used = image_pos >= 0
    last_slot = jnp.maximum(jnp.max(jnp.where(slot_used, slot_ids, -1)), 0)
    last_pos = jnp.max(jnp.where(slot_used, image_pos, -1))
    local_keys = jnp.dot(latents, key_panel, preferred_element_type=jnp.float32).astype(
        jnp.bfloat16
    )
    local_values = jnp.dot(latents, value_panel, preferred_element_type=jnp.float32).astype(
        jnp.bfloat16
    )
    last_key = lax.dynamic_slice_in_dim(local_keys, last_slot * lat_rows, lat_rows, 0)
    last_value = lax.dynamic_slice_in_dim(local_values, last_slot * lat_rows, lat_rows, 0)
    identity = (jnp.int32(-1), jnp.zeros_like(last_key), jnp.zeros_like(last_value))
    carried_pos, carried_key, carried_value = carried_in(
        (last_pos, last_key, last_value), "ctx", take_newer, identity
    )
    all_keys = jnp.concatenate([carried_key, local_keys], axis=0)
    all_values = jnp.concatenate([carried_value, local_values], axis=0)
    cand_pos = jnp.concatenate([jnp.reshape(carried_pos, (1,)), image_pos]).astype(jnp.int32)
    cand_ids = jnp.arange(slot_count + 1, dtype=jnp.int32)
    position = lax.axis_index("ctx") * tok_rows + jnp.arange(tok_rows, dtype=jnp.int32)
    eligible = (cand_pos[None, :] >= 0) & (cand_pos[None, :] <= position[:, None])
    chosen = jnp.max(jnp.where(eligible, cand_ids[None, :], -1), axis=1)
    chosen_pos = jnp.max(jnp.where(eligible, cand_pos[None, :], -1), axis=1)
    starts = jnp.cumsum(doc_lengths) - doc_lengths
    doc_start = jnp.max(jnp.where(starts[None, :] <= position[:, None], starts[None, :], 0), axis=1)
    gate_open = (chosen >= 0) & (chosen_pos >= doc_start)
    latent_image = jnp.arange((slot_count + 1) * lat_rows, dtype=jnp.int32) // lat_rows
    head_count = queries.shape[1] // HEAD_DIM
    query_heads = queries.reshape(tok_rows, head_count, HEAD_DIM)
    key_heads = all_keys.reshape(all_keys.shape[0], head_count, HEAD_DIM)
    value_heads = all_values.reshape(all_values.shape[0], head_count, HEAD_DIM)
    score_scale = 1.0 / HEAD_DIM**0.5
    scores = (
        jnp.einsum("thd,khd->htk", query_heads, key_heads, preferred_element_type=jnp.float32)
        * score_scale
    )
    allowed = latent_image[None, :] == chosen[:, None]
    scores = jnp.where(allowed[None, :, :], scores, jnp.float32(-1e30))
    probs = jax.nn.softmax(scores, axis=-1).astype(jnp.bfloat16)
    attended = jnp.einsum("htk,khd->thd", probs, value_heads, preferred_element_type=jnp.float32)
    attended = attended.reshape(tok_rows, head_count * HEAD_DIM).astype(jnp.bfloat16)
    partial_terms = jnp.dot(attended, out_panel, preferred_element_type=jnp.float32)
    branch = lax.psum_scatter(
        partial_terms.astype(jnp.bfloat16), "shard", scatter_dimension=1, tiled=True
    ).astype(jnp.float32)
    factor = jnp.tanh(alpha[0]) * gate_open.astype(jnp.float32)
    return (tokens.astype(jnp.float32) + factor[:, None] * branch).astype(jnp.bfloat16)


def solution(mesh):
    in_specs = (
        P(("groups", "ctx"), "shard"),
        P("shard"),
        P("ctx", "shard"),
        P("ctx", "shard"),
        P("ctx", "shard"),
        P("shard", "ctx"),
        P(("groups", "ctx"), None),
        P(("groups", "ctx")),
        P("groups"),
        P(),
    )
    out_specs = P(("groups", "ctx"), "shard")
    return jax.shard_map(body, mesh=mesh, in_specs=in_specs, out_specs=out_specs, check_vma=False)
```

profile of v0, /device:TPU:3, one launch (start us, length us, event | category | flops | bytes accessed | tf_op | source)
XLA Modules:
  0.0 457.0 jit_solution(11762009155505323417)
XLA Ops:
  6.5 0.7 all-gather.8.cloned.1.call-update
  7.3 0.7 all-gather.10.cloned.1.call-update
  8.1 0.7 all-gather.12.cloned.1.call-update
  10.0 0.7 dynamic-slice
  11.3 1.4 dynamic-update-slice
  12.7 3.1 all-reduce
  16.5 10.6 %all_gather.45 = bf16[8192]{0:T(1024)(128)(2,1)S(1)} all-gather(bf16[2048]{0:T(1024)(128)(2,1)S(1)} %copy-done.3), channel_id=1, replica_groups=mesh['groups'=2,'ctx'=4,'shard'=4] {'shard'}, dimensions={0}, use_global_device_ids=true | all-gather | bytes 20480 | tf_op jit(solution)/shard_map/all_gather | solution.py:37
  27.1 7.9 %all-gather.8.cloned.1.call-done = bf16[1280,1024]{1,0:T(8,128)(2,1)} async-done(((bf16[320,1024]{1,0:T(8,128)(2,1)}), bf16[1280,1024]{1,0:T(8,128)(2,1)}) %all-gather.8.cloned.1.call-update) | async-done | bytes 2621456 | tf_op jit(solution)/shard_map/all_gather | solution.py:45
  35.0 2.6 convolution_convert_fusion.2
  37.6 24.5 %all-gather.10.cloned.1.call-done = bf16[1280,1024]{1,0:T(8,128)(2,1)} async-done(((bf16[320,1024]{1,0:T(8,128)(2,1)}), bf16[1280,1024]{1,0:T(8,128)(2,1)}) %all-gather.10.cloned.1.call-update) | async-done | bytes 2621456 | tf_op jit(solution)/shard_map/all_gather | solution.py:46
  62.1 2.6 convolution_convert_fusion.1
  64.8 7.5 %all-gather = bf16[256,1024]{1,0:T(8,128)(2,1)S(1)} all-gather(bf16[64,1024]{1,0:T(8,128)(2,1)S(1)} %constant_dynamic-slice_fusion.1), channel_id=2, replica_groups=mesh['groups'=2,'ctx'=4,'shard'=4] {'ctx'}, dimensions={0}, use_global_device_ids=true | all-gather | bytes 655360 | tf_op jit(solution)/shard_map/all_gather | solution.py:11
  72.3 7.5 %all-gather.1 = bf16[256,1024]{1,0:T(8,128)(2,1)S(1)} all-gather(bf16[64,1024]{1,0:T(8,128)(2,1)S(1)} %constant_dynamic-slice_fusion), channel_id=3, replica_groups=mesh['groups'=2,'ctx'=4,'shard'=4] {'ctx'}, dimensions={0}, use_global_device_ids=true | all-gather | bytes 655360 | tf_op jit(solution)/shard_map/all_gather | solution.py:11
  79.7 6.0 %while.18 = (s32[]{:T(128)}, s32[]{:T(128)}, bf16[64,1024]{1,0:T(8,128)(2,1)S(1)}, bf16[64,1024]{1,0:T(8,128)(2,1)S(1)}, s32[]{:T(128)}, /*index=5*/s32[4]{0:T(1...) while((s32[]{:T(128)}, s32[]{:T(128)}, ...), condition=%wide.region_3.4_spmd.clone, body=%wide.region_2.3_spmd.clone.sunk | while | flops 393223 | bytes 786605 | solution.py:20
  86.1 59.2 %all-gather.12.cloned.1.call-done = bf16[256,8192]{1,0:T(8,128)(2,1)} async-done(((bf16[256,2048]{1,0:T(8,128)(2,1)}), bf16[256,8192]{1,0:T(8,128)(2,1)}) %all-gather.12.cloned.1.call-update) | async-done | bytes 4194320 | tf_op jit(solution)/shard_map/all_gather | solution.py:36
  145.3 3.1 fusion.1
  148.4 102.0 %all-gather.14.cloned.1.call-done = bf16[8192,1024]{1,0:T(8,128)(2,1)} async-done(((bf16[2048,1024]{1,0:T(8,128)(2,1)}), bf16[8192,1024]{1,0:T(8,128)(2,1)}) %all-gather.14.cloned.1.call-update) | async-done | bytes 16777232 | tf_op jit(solution)/shard_map/all_gather | solution.py:49
  250.4 11.6 %fusion.17 = bf16[32,8,8,128]{3,2,1,0:T(8,128)(2,1)S(1)} fusion(bf16[8192,1024]{1,0:T(8,128)(2,1)} %all-gather.14.cloned.1.call-done, bf16[256,8192]{1,0:T(8,128)(2,1)} %all-gather.12.cloned.1.call-done, f32[8192]{0:T(1024)S(1)} %convert_element_type.47, f32[256]{0:T(256)S(1)} %add_rsqrt_fusion), kind=kOutput, calls=%fused_computation.25 | convolution fusion | flops 4303618048 | bytes 21529600 | tf_op jit(solution)/shard_map/dot_general | solution.py:52
  262.0 2.5 fusion.46
  264.6 2.8 fusion.16
  267.4 90.4 %all-gather.16.cloned.1.call-done = bf16[1024,8192]{1,0:T(8,128)(2,1)} async-done(((bf16[1024,2048]{1,0:T(8,128)(2,1)}), bf16[1024,8192]{1,0:T(8,128)(2,1)}) %all-gather.16.cloned.1.call-update) | async-done | bytes 16777232 | tf_op jit(solution)/shard_map/all_gather | solution.py:50
  357.8 12.0 %convolution_convert_fusion = bf16[256,8192]{1,0:T(8,128)(2,1)} fusion(bf16[256,1024]{0,1:T(8,128)(2,1)S(1)} %bitcast.66, bf16[1024,8192]{1,0:T(8,128)(2,1)} %all-gather.16.cloned.1.call-done), kind=kOutput, calls=%fused_computation.5 | convolution fusion | flops 4297064448 | bytes 21495808 | tf_op jit(solution)/shard_map/dot_general | solution.py:97
  371.5 76.1 %reduce-scatter.2.cloned.1.call-done = bf16[256,2048]{1,0:T(8,128)(2,1)} async-done(((bf16[256,8192]{1,0:T(8,128)(2,1)}), bf16[256,2048]{1,0:T(8,128)(2,1)}) %reduce-scatter.2.cloned.1.call-update) | async-done | bytes 1048592 | tf_op jit(solution)/shard_map/reduce_scatter | solution.py:98
  447.6 2.6 add_convert_fusion
  (46 shorter events, 5.4 us)
Async XLA Ops:
  6.5 28.5 %copy-start = (bf16[256,1280]{1,0:T(8,128)(2,1)S(1)}, bf16[256,1280]{1,0:T(8,128)(2,1)}, u32[]{:S(2)}) copy-start(bf16[256,1280]{1,0:T(8,128)(2,1)} %param.18) | copy-start | bytes 1966084
  6.5 28.5 %all-gather.8.cloned.1.call-start = ((), (), s32[]{:S(2)}) async-start(), calls=%async_computation.1 | async-start | bytes 3276800 | tf_op jit(solution)/shard_map/all_gather | solution.py:45
  7.3 54.9 %all-gather.10.cloned.1.call-start = ((), (), s32[]{:S(2)}) async-start(), calls=%async_computation.2 | async-start | bytes 3276800 | tf_op jit(solution)/shard_map/all_gather | solution.py:46
  8.0 137.3 %all-gather.12.cloned.1.call-start = ((), (), s32[]{:S(2)}) async-start(), calls=%async_computation.3 | async-start | bytes 5242880 | tf_op jit(solution)/shard_map/all_gather | solution.py:36
  8.7 241.7 %all-gather.14.cloned.1.call-start = ((), (), s32[]{:S(2)}) async-start(), calls=%async_computation.4 | async-start | bytes 20971520 | tf_op jit(solution)/shard_map/all_gather | solution.py:49
  9.3 0.7 copy-start.6
  9.3 1.3 copy-start.4
  9.3 7.1 %copy-start.3 = (bf16[2048]{0:T(1024)(128)(2,1)S(1)}, bf16[2048]{0:T(1024)(128)(2,1)}, u32[]{:S(2)}) copy-start(bf16[2048]{0:T(1024)(128)(2,1)} %param.13) | copy-start | bytes 12292
  9.4 348.5 %all-gather.16.cloned.1.call-start = ((), (), s32[]{:S(2)}) async-start(), calls=%async_computation.5 | async-start | bytes 20971520 | tf_op jit(solution)/shard_map/all_gather | solution.py:50
  9.9 437.6 %reduce-scatter.2.cloned.1.call-start = ((), (), s32[]{:S(2)}) async-start(), calls=%async_computation.6 | async-start | bytes 5242880 | tf_op jit(solution)/shard_map/reduce_scatter | solution.py:98
  369.8 0.7 copy-start.5
  369.8 77.7 %copy-start.2 = (bf16[256,2048]{1,0:T(8,128)(2,1)S(1)}, bf16[256,2048]{1,0:T(8,128)(2,1)}, u32[]{:S(2)}) copy-start(bf16[256,2048]{1,0:T(8,128)(2,1)} %param.12) | copy-start | bytes 3145732
  369.9 80.3 %copy-start.1 = (bf16[256,1280]{1,0:T(8,128)(2,1)S(1)}, bf16[256,1280]{1,0:T(8,128)(2,1)}, u32[]{:S(2)}) copy-start(bf16[256,1280]{1,0:T(8,128)(2,1)} %param.18) | copy-start | bytes 1966084
Sparse Core Ops, SparseCore 0:
  8.9 26.0 all-gather.7
  36.5 25.5 all-gather.9
  63.7 81.5 all-gather.11
  146.7 103.7 all-gather.13
  251.8 105.9 all-gather.15
  370.0 77.5 reduce-scatter.1
where the time goes:
time: 459 us; the launch traced here: 457 us
  waiting for transfers between devices  363 us (79%)
  matrix products  34.1 us (7%)
  blocking collectives  28.7 us (6%)
  between operations  15 us (3%)
  other arithmetic  7.31 us (2%)
    all_gather x1, waiting for transfers between devices, body(): lax.all_gather(w_query, 'ctx', axis=0, tiled=True)  102 us
    all_gather x1, waiting for transfers between devices, body(): lax.all_gather(w_out, 'ctx', axis=1, tiled=True)  90.4 us
    reduce_scatter x1, waiting for transfers between devices, body(): lax.psum_scatter(partial_terms.astype(jnp.bfloat16), 'shard', scatter_dim...  76.1 us
    all_gather x1, waiting for transfers between devices, body(): lax.all_gather(tokens, 'shard', axis=1, tiled=True)  59.2 us
    all_gather x1, waiting for transfers between devices, body(): lax.all_gather(w_value, 'ctx', axis=0, tiled=True)  24.5 us
    all_gather x2, blocking collectives, carried_in(): pieces = jax.tree.map(lambda part: lax.all_gather(part, axis), value)  15 us
    dot_general x1, matrix products, body(): jnp.dot(attended, out_panel, preferred_element_type=jnp.float32)  12 us
    dot_general x1, matrix products, body(): jnp.dot(normed, query_panel, preferred_element_type=jnp.float32)  11.6 us
  transfers between devices with their start and end apart: 6, of which 6 were waited for; matrix products, arithmetic and copies ran while one was open for 7% of the time, Pallas kernels for 0%

commit v1 on v0

v1 whole, which is shorter than its diff:
```python
import jax
import jax.numpy as jnp
from jax import lax
from jax.sharding import PartitionSpec as P

HEAD_DIM = 128


FLIP_FAR = [(0, 2), (1, 3), (2, 0), (3, 1)]
FLIP_NEAR = [(0, 1), (1, 0), (2, 3), (3, 2)]
FLIP_GROUP = [(0, 1), (1, 0)]


def gathered_panels(panel, chunks):
    mine, group = lax.axis_index("ctx"), lax.axis_index("groups")
    half = panel.shape[0] // 2
    size = half // chunks
    near_owner, far_owner, diagonal = mine ^ 1, mine ^ 2, mine ^ 3
    pieces = [(mine, 0, panel), (near_owner, 0, lax.ppermute(panel, "ctx", FLIP_NEAR))]
    for chunk in range(chunks):
        first = group * half + chunk * size
        other_first = (1 - group) * half + chunk * size
        sent = lax.dynamic_slice_in_dim(panel, first, size, 0)
        direct = lax.ppermute(sent, "ctx", FLIP_FAR)
        handed = lax.ppermute(direct, "groups", FLIP_GROUP)
        pieces.append((far_owner, first, direct))
        pieces.append((far_owner, other_first, handed))
        pieces.append((diagonal, first, lax.ppermute(direct, "ctx", FLIP_NEAR)))
        pieces.append((diagonal, other_first, lax.ppermute(handed, "ctx", FLIP_NEAR)))
    return pieces


def whole_panel(panel, axis_size, chunks=1):
    if axis_size != 4:
        return lax.all_gather(panel, "ctx", axis=0, tiled=True)
    rows = panel.shape[0]
    whole = jnp.zeros((rows * 4, panel.shape[1]), panel.dtype)
    for owner, first, part in gathered_panels(panel, chunks):
        whole = lax.dynamic_update_slice_in_dim(whole, part, owner * rows + first, 0)
    return whole


def project_in(normed, panel, axis_size):
    if axis_size != 4:
        whole = lax.all_gather(panel, "ctx", axis=0, tiled=True)
        return jnp.dot(normed, whole, preferred_element_type=jnp.float32)
    total = 0.0
    for owner, first, part in gathered_panels(panel, 2):
        start = owner * panel.shape[0] + first
        columns = lax.dynamic_slice_in_dim(normed, start, part.shape[0], 1)
        total = total + jnp.dot(columns, part, preferred_element_type=jnp.float32)
    return total


def project_out(attended, panel, axis_size):
    if axis_size != 4:
        whole = lax.all_gather(panel, "ctx", axis=1, tiled=True)
        return jnp.dot(attended, whole, preferred_element_type=jnp.float32).astype(jnp.bfloat16)
    width = panel.shape[1]
    whole = jnp.zeros((attended.shape[0], 4 * width), jnp.bfloat16)
    by_owner = {}
    for place, (owner, first, part) in enumerate(gathered_panels(panel, 2)):
        key = place if place < 2 else 2 + (place - 2) % 4 // 2
        by_owner.setdefault(key, []).append((owner, first, part))
    for parts in by_owner.values():
        total = 0.0
        for owner, first, part in parts:
            rows = lax.dynamic_slice_in_dim(attended, first, part.shape[0], 1)
            total = total + jnp.dot(rows, part, preferred_element_type=jnp.float32)
        whole = lax.dynamic_update_slice_in_dim(
            whole, total.astype(jnp.bfloat16), parts[0][0] * width, 1
        )
    return whole


def latest_before(image_pos, latents, lat_rows):
    count, mine = lax.axis_size("ctx"), lax.axis_index("ctx")
    slot_ids = jnp.arange(image_pos.shape[0], dtype=jnp.int32)
    used = image_pos >= 0
    last_slot = jnp.maximum(jnp.max(jnp.where(used, slot_ids, -1)), 0)
    last_pos = jnp.max(jnp.where(used, image_pos, -1))
    last_rows = lax.dynamic_slice_in_dim(latents, last_slot * lat_rows, lat_rows, 0)
    column = jnp.arange(latents.shape[1], dtype=jnp.int32)[None, :]
    digits = jnp.where(column == 0, last_pos // 64, jnp.where(column == 1, last_pos % 64, 0))
    tag = jnp.broadcast_to(digits, (16, latents.shape[1])).astype(jnp.bfloat16)
    blocks = lax.all_gather(jnp.concatenate([last_rows, tag], axis=0), "ctx")
    places = blocks[:, lat_rows, :2].astype(jnp.int32)
    places = places[:, 0] * 64 + places[:, 1]
    before = jnp.arange(count, dtype=jnp.int32) < mine
    pos = jnp.max(jnp.where(before, places, -1))
    source = jnp.argmax(jnp.where(before, places, -1))
    rows = lax.dynamic_index_in_dim(blocks, source, 0, keepdims=False)[:lat_rows]
    return pos, rows


def body(tokens, gain, w_query, w_key, w_value, w_out, latents, image_pos, doc_lengths, alpha):
    n_ctx = lax.axis_size("ctx")
    tok_rows = tokens.shape[0]
    slot_count = image_pos.shape[0]
    lat_rows = latents.shape[0] // slot_count
    carried_pos, carried_rows = latest_before(image_pos, latents, lat_rows)
    gathered = lax.all_gather(tokens, "shard", axis=1, tiled=True)
    full_gain = lax.all_gather(gain, "shard", axis=0, tiled=True)
    widened = gathered.astype(jnp.float32)
    mean_square = jnp.mean(widened * widened, axis=-1, keepdims=True)
    normed = (widened * lax.rsqrt(mean_square + 1e-06) * full_gain.astype(jnp.float32)).astype(
        jnp.bfloat16
    )
    kv_panel = whole_panel(jnp.concatenate([w_key, w_value], axis=1), n_ctx)
    all_latents = jnp.concatenate([carried_rows, latents], axis=0)
    all_kv = jnp.dot(all_latents, kv_panel, preferred_element_type=jnp.float32).astype(jnp.bfloat16)
    all_keys, all_values = jnp.split(all_kv, 2, axis=1)
    queries = project_in(normed, w_query, n_ctx).astype(jnp.bfloat16)
    cand_pos = jnp.concatenate([jnp.reshape(carried_pos, (1,)), image_pos]).astype(jnp.int32)
    cand_ids = jnp.arange(slot_count + 1, dtype=jnp.int32)
    position = lax.axis_index("ctx") * tok_rows + jnp.arange(tok_rows, dtype=jnp.int32)
    eligible = (cand_pos[None, :] >= 0) & (cand_pos[None, :] <= position[:, None])
    chosen = jnp.max(jnp.where(eligible, cand_ids[None, :], -1), axis=1)
    chosen_pos = jnp.max(jnp.where(eligible, cand_pos[None, :], -1), axis=1)
    starts = jnp.cumsum(doc_lengths) - doc_lengths
    doc_start = jnp.max(jnp.where(starts[None, :] <= position[:, None], starts[None, :], 0), axis=1)
    gate_open = (chosen >= 0) & (chosen_pos >= doc_start)
    latent_image = jnp.arange((slot_count + 1) * lat_rows, dtype=jnp.int32) // lat_rows
    head_count = queries.shape[1] // HEAD_DIM
    query_heads = queries.reshape(tok_rows, head_count, HEAD_DIM)
    key_heads = all_keys.reshape(all_keys.shape[0], head_count, HEAD_DIM)
    value_heads = all_values.reshape(all_values.shape[0], head_count, HEAD_DIM)
    score_scale = 1.0 / HEAD_DIM**0.5
    scores = (
        jnp.einsum("thd,khd->htk", query_heads, key_heads, preferred_element_type=jnp.float32)
        * score_scale
    )
    allowed = latent_image[None, :] == chosen[:, None]
    scores = jnp.where(allowed[None, :, :], scores, jnp.float32(-1e30))
    probs = jax.nn.softmax(scores, axis=-1).astype(jnp.bfloat16)
    attended = jnp.einsum("htk,khd->thd", probs, value_heads, preferred_element_type=jnp.float32)
    attended = attended.reshape(tok_rows, head_count * HEAD_DIM).astype(jnp.bfloat16)
    partial_terms = project_out(attended, w_out, n_ctx)
    branch = lax.psum_scatter(partial_terms, "shard", scatter_dimension=1, tiled=True).astype(
        jnp.float32
    )
    factor = jnp.tanh(alpha[0]) * gate_open.astype(jnp.float32)
    return (tokens.astype(jnp.float32) + factor[:, None] * branch).astype(jnp.bfloat16)


def solution(mesh):
    in_specs = (
        P(("groups", "ctx"), "shard"),
        P("shard"),
        P("ctx", "shard"),
        P("ctx", "shard"),
        P("ctx", "shard"),
        P("shard", "ctx"),
        P(("groups", "ctx"), None),
        P(("groups", "ctx")),
        P("groups"),
        P(),
    )
    out_specs = P(("groups", "ctx"), "shard")
    return jax.shard_map(body, mesh=mesh, in_specs=in_specs, out_specs=out_specs, check_vma=False)
```

time: 459 us -> 328 us (0.71)
  waiting for transfers between devices: 363 us -> 140 us
  blocking collectives: 28.7 us -> 70.4 us
  local copies, waits for them, and re-layouts: 4.5 us -> 23.7 us
  starting transfers between devices: 0.19 us -> 17.7 us
  matrix products: 34.1 us -> 43.5 us
    all_gather x5 -> x1, waiting for transfers between devices: 284 us -> 0.01 us  [body(): gathered = lax.all_gather(tokens, 'shard', axis=1, tiled=True)]
    ppermute x0 -> x23, waiting for transfers between devices: none -> 63.9 us  [the longest x5 43.9 us: gathered_panels(): handed = lax.ppermute(direct, 'groups', FLIP_GROUP)]
    all_gather x3 -> x2, blocking collectives: 25.6 us -> 70.4 us  [the longest x1 59.7 us: latest_before(): blocks = lax.all_gather(jnp.concatenate([last_rows, tag], axis=0), 'ctx')]
    ppermute x0 -> x23, starting transfers between devices: none -> 17.7 us  [the longest x5 7.47 us: gathered_panels(): pieces.append((diagonal, first, lax.ppermute(direct, 'ctx', FLIP_NEAR)))]
    dot_general x4 -> x21, matrix products: 28.8 us -> 37.3 us  [the longest x10 21.2 us: project_out(): total = total + jnp.dot(rows, part, preferred_element_type=jnp.float32)]
    dynamic_update_slice x0 -> x6, local copies, waits for them, and re-layouts: none -> 6.97 us  [whole_panel(): lax.dynamic_update_slice_in_dim(whole, part, owner * rows + first, 0)]
    dynamic_slice x5 -> x4, local copies, waits for them, and re-layouts: 1.82 us -> 8.04 us  [the longest x3 7.08 us: gathered_panels(): sent = lax.dynamic_slice_in_dim(panel, first, size, 0)]
    broadcast_in_dim x0 -> x3, local copies, waits for them, and re-layouts: none -> 5.4 us  [the longest x1 2.96 us: whole_panel(): whole = jnp.zeros((rows * 4, panel.shape[1]), panel.dtype)]
  transfers between devices with their start and end apart: 6 -> 25, of which waited for: 6 -> 6; matrix products, arithmetic and copies ran while one was open for 7% -> 22% of each run, Pallas kernels for 0% -> 0%
where the time goes in v1:
time: 328 us; the launch traced here: 325 us
  waiting for transfers between devices  140 us (43%)
  blocking collectives  70.4 us (21%)
  matrix products  43.5 us (13%)
  local copies, waits for them, and re-layouts  23.7 us (7%)
  between operations  19.4 us (6%)
  starting transfers between devices  17.7 us (5%)
  other arithmetic  10.3 us (3%)
    reduce_scatter x1, waiting for transfers between devices, body(): lax.psum_scatter(partial_terms, 'shard', scatter_dimension=1, tiled=True)  75.9 us
    all_gather x1, blocking collectives, latest_before(): blocks = lax.all_gather(jnp.concatenate([last_rows, tag], axis=0), 'ctx')  59.7 us
    ppermute x5, waiting for transfers between devices, gathered_panels(): handed = lax.ppermute(direct, 'groups', FLIP_GROUP)  43.9 us
    dot_general x10, matrix products, project_out(): total = total + jnp.dot(rows, part, preferred_element_type=jnp.float32)  21.2 us
    ppermute x5, waiting for transfers between devices, gathered_panels(): direct = lax.ppermute(sent, 'ctx', FLIP_FAR)  20 us
    dot_general x10, matrix products, project_in(): total = total + jnp.dot(columns, part, preferred_element_type=jnp.float32)  11.7 us
    all_gather x1, blocking collectives, body(): full_gain = lax.all_gather(gain, 'shard', axis=0, tiled=True)  10.6 us
    ppermute x5, starting transfers between devices, gathered_panels(): pieces.append((diagonal, first, lax.ppermute(direct, 'ctx', FLIP_NEAR)))  7.47 us
  transfers between devices with their start and end apart: 25, of which 6 were waited for; matrix products, arithmetic and copies ran while one was open for 22% of the time, Pallas kernels for 0%

profile of v1, /device:TPU:3, one launch (start us, length us, event | category | flops | bytes accessed | tf_op | source)
XLA Modules:
  0.0 325.4 jit_solution(12659103084228882540)
XLA Ops:
  8.1 3.0 constant_dynamic-slice_fusion.3
  18.8 59.7 %all-gather = bf16[320,1280]{1,0:T(8,128)(2,1)S(1)} all-gather(bf16[80,1280]{1,0:T(8,128)(2,1)S(1)} %pad_maximum_fusion), channel_id=2, replica_groups=mesh['groups'=2,'ctx'=4,'shard'=4] {'ctx'}, dimensions={0}, use_global_device_ids=true | all-gather | bytes 1024000 | tf_op jit(solution)/shard_map/all_gather | solution.py:86
  83.4 3.0 broadcast_in_dim.91
  89.1 10.6 %all_gather.15 = bf16[8192]{0:T(1024)(128)(2,1)S(1)} all-gather(bf16[2048]{0:T(1024)(128)(2,1)S(1)} %copy-done.8), channel_id=1, replica_groups=mesh['groups'=2,'ctx'=4,'shard'=4] {'shard'}, dimensions={0}, use_global_device_ids=true | all-gather | bytes 20480 | tf_op jit(solution)/shard_map/all_gather | solution.py:103
  99.7 3.1 constant_dynamic-slice_fusion.1
  102.9 3.4 %collective-permute-start.3 = (bf16[160,2048]{1,0:T(8,128)(2,1)}, bf16[160,2048]{1,0:T(8,128)(2,1)S(1)}, u32[]{:S(2)}, u32[]{:S(2)}) collective-permute-start(bf16[160,2048]{1,0:T(8,128)(2,1)} %collective-permute-done.1), channel_id=1, source_target_pairs={{0,4},{4,0},{8,12},{12,8},{1,5},{5,1},{9,13},{13,9},{2,6},{6,2},{1... | collective-permute-start | bytes 1966088 | tf_op jit(solution)/shard_map/ppermute | solution.py:28
  107.5 2.0 constant_dynamic-update-slice_fusion.3
  113.4 4.4 %convolution_convert_fusion = bf16[320,2048]{1,0:T(8,128)(2,1)S(1)} fusion(bf16[1280,2048]{1,0:T(8,128)(2,1)} %constant_dynamic-update-slice_fusion, bf16[256,1280]{1,0:T(8,128)(2,1)S(1)} %copy-done.7, bf16[64,1280]{1,0:T(8,128)(2,1)S(1)} %copy-done.6), kind=kOutput, calls=%fused_computation.12 | convolution fusion | flops 1680015360 | bytes 7372800 | tf_op jit(solution)/shard_map/dot_general | solution.py:111
  119.0 3.3 fusion.1
  127.2 7.8 %collective-permute-done.17 = bf16[256,2048]{1,0:T(8,128)(2,1)} collective-permute-done((bf16[256,2048]{1,0:T(8,128)(2,1)}, bf16[256,2048]{1,0:T(8,128)(2,1)}, u32[]{:S(2)}, u32[]{:S(2)}) %collective-permute-start.17) | collective-permute-done | bytes 1048608 | tf_op jit(solution)/shard_map/ppermute | solution.py:24
  135.0 2.1 collective-permute-start.12
  139.1 3.5 %convolution_add_fusion.9 = f32[256,1024]{1,0:T(8,128)S(1)} fusion(f32[256,1024]{1,0:T(8,128)S(1)} %fusion.24, bf16[2048,1024]{1,0:T(8,128)(2,1)} %collective-permute-done.5, bf16[256,8192]{1,0:T(8,128)(2,1)S(1)} %fusion.3, s32[]{:T(128)S(6)} %select_n.179), kind=kOutput, calls=%fused_computation.38 | convolution fusion | flops 1074003968 | bytes 7340036 | tf_op jit(solution)/shard_map/dot_general | solution.py:51
  145.3 12.1 %collective-permute-done.15 = bf16[256,2048]{1,0:T(8,128)(2,1)} collective-permute-done((bf16[256,2048]{1,0:T(8,128)(2,1)S(1)}, bf16[256,2048]{1,0:T(8,128)(2,1)}, u32[]{:S(2)}, u32[]{:S(2)}) %collective-permute-start.15) | collective-permute-done | bytes 1048608 | tf_op jit(solution)/shard_map/ppermute | solution.py:24
  159.0 3.2 collective-permute-done.11
  165.3 19.5 %collective-permute-done.16 = bf16[256,2048]{1,0:T(8,128)(2,1)} collective-permute-done((bf16[256,2048]{1,0:T(8,128)(2,1)}, bf16[256,2048]{1,0:T(8,128)(2,1)}, u32[]{:S(2)}, u32[]{:S(2)}) %collective-permute-start.16) | collective-permute-done | bytes 1048608 | tf_op jit(solution)/shard_map/ppermute | solution.py:25
  185.9 21.2 %collective-permute-done.18 = bf16[256,2048]{1,0:T(8,128)(2,1)S(1)} collective-permute-done((bf16[256,2048]{1,0:T(8,128)(2,1)}, bf16[256,2048]{1,0:T(8,128)(2,1)S(1)}, u32[]{:S(2)}, u32[]{:S(2)}) %collective-permute-start.18) | collective-permute-done | bytes 1048608 | tf_op jit(solution)/shard_map/ppermute | solution.py:25
  209.1 3.8 %fusion.98 = (f32[8,256]{1,0:T(8,128)S(1)}, f32[8,256,320]{1,2,0:T(8,128)}) fusion(pred[256,320]{0,1:T(8,128)(4,1)S(1)} %broadcast_compare_fusion, bf16[40,8,8,128]{3,2,1,0:T(8,128)(2,1)} %get-tuple-element.20, bf16[32,8,8,128]{3,2,1,0:T(8,128)(2,1)} %fusion.22), kind=kOutput, calls=%fused_computation.146 | convolution fusion | flops 170393920 | bytes 3891200 | tf_op jit(solution)/shard_map/sub | solution.py:135
  213.0 2.4 fusion.21
  217.1 1.9 fusion.65
  220.8 2.4 broadcast_in_dim.90
  223.2 4.5 %fusion.11 = bf16[256,8192]{1,0:T(8,128)(2,1)} fusion(bf16[256,8192]{1,0:T(8,128)(2,1)} %broadcast_in_dim.90, s32[]{:T(128)S(6)} %select_n.178, bf16[256,1024]{0,1:T(8,128)(2,1)S(1)} %bitcast.74, bf16[1024,2048]{1,0:T(8,128)(2,1)} %param.15), kind=kOutput, calls=%fused_computation.23 | convolution fusion | flops 1074266112 | bytes 5767172 | tf_op jit(solution)/shard_map/dot_general | solution.py:69
  227.7 4.5 %fusion.10 = bf16[256,8192]{1,0:T(8,128)(2,1)} fusion(bf16[256,8192]{1,0:T(8,128)(2,1)} %fusion.11, s32[]{:T(128)S(6)} %select_n.179, bf16[256,1024]{0,1:T(8,128)(2,1)S(1)} %bitcast.75, bf16[1024,2048]{1,0:T(8,128)(2,1)} %collective-permute-done.14), kind=kOutput, calls=%fused_computation.21 | convolution fusion | flops 1074266112 | bytes 5767172 | tf_op jit(solution)/shard_map/dot_general | solution.py:69
  240.1 75.9 %reduce-scatter.2.cloned.1.call-done = bf16[256,2048]{1,0:T(8,128)(2,1)} async-done(((bf16[256,8192]{1,0:T(8,128)(2,1)}), bf16[256,2048]{1,0:T(8,128)(2,1)}) %reduce-scatter.2.cloned.1.call-update) | async-done | bytes 1048592 | tf_op jit(solution)/shard_map/reduce_scatter | solution.py:139
  316.0 2.6 add_convert_fusion
  (114 shorter events, 46.0 us)
Async XLA Ops:
  6.5 112.4 %all-gather.3.cloned.1.call-start = ((), (), s32[]{:S(2)}) async-start(), calls=%async_computation.1 | async-start | bytes 5242880 | tf_op jit(solution)/shard_map/all_gather | solution.py:102
  7.3 308.7 %reduce-scatter.2.cloned.1.call-start = ((), (), s32[]{:S(2)}) async-start(), calls=%async_computation.2 | async-start | bytes 5242880 | tf_op jit(solution)/shard_map/reduce_scatter | solution.py:139
  7.3 129.8 %collective-permute-start.5 = (bf16[2048,1024]{1,0:T(8,128)(2,1)}, bf16[2048,1024]{1,0:T(8,128)(2,1)}, u32[]{:S(2)}, u32[]{:S(2)}) collective-permute-start(bf16[2048,1024]{1,0:T(8,128)(2,1)} %param.12), channel_id=1, source_target_pairs={{0,4},{4,0},{8,12},{12,8},{1,5},{5,1},{9,13},{13,9},{2,6},{6,2},{1... | collective-permute-start | bytes 12582920 | tf_op jit(solution)/shard_map/ppermute | solution.py:19
  11.1 99.3 %collective-permute-start.6 = (bf16[512,1024]{1,0:T(8,128)(2,1)}, bf16[512,1024]{1,0:T(8,128)(2,1)}, u32[]{:S(2)}, u32[]{:S(2)}) collective-permute-start(bf16[512,1024]{1,0:T(8,128)(2,1)} %get-tuple-element.17), channel_id=1, source_target_pairs={{0,8},{4,12},{8,0},{12,4},{1,9},{5,13},{9,1},{13,5},{2,10},{6,14},... | collective-permute-start | bytes 3145736 | tf_op jit(solution)/shard_map/ppermute | solution.py:24
  11.1 114.8 %collective-permute-start.10 = (bf16[512,1024]{1,0:T(8,128)(2,1)}, bf16[512,1024]{1,0:T(8,128)(2,1)}, u32[]{:S(2)}, u32[]{:S(2)}) collective-permute-start(bf16[512,1024]{1,0:T(8,128)(2,1)} %get-tuple-element.18), channel_id=1, source_target_pairs={{0,8},{4,12},{8,0},{12,4},{1,9},{5,13},{9,1},{13,5},{2,10},{6,14},... | collective-permute-start | bytes 3145736 | tf_op jit(solution)/shard_map/ppermute | solution.py:24
  12.7 90.2 %collective-permute-start = (bf16[320,2048]{1,0:T(8,128)(2,1)S(1)}, bf16[320,2048]{1,0:T(8,128)(2,1)S(1)}, u32[]{:S(2)}, u32[]{:S(2)}) collective-permute-start(bf16[320,2048]{1,0:T(8,128)(2,1)S(1)} %constant_dynamic-update-slice_fusion.6), channel_id=1, source_target_pairs={{0,4},{4,0},{8,12},{12,8},{1,5},{5,1},{9,13},{13,9},{2,6},{6,2},{1... | collective-permute-start | bytes 3932168 | tf_op jit(solution)/shard_map/ppermute | solution.py:19
  14.2 73.3 %collective-permute-start.1 = (bf16[160,2048]{1,0:T(8,128)(2,1)}, bf16[160,2048]{1,0:T(8,128)(2,1)}, u32[]{:S(2)}, u32[]{:S(2)}) collective-permute-start(bf16[160,2048]{1,0:T(8,128)(2,1)} %constant_dynamic-slice_fusion.4), channel_id=1, source_target_pairs={{0,8},{4,12},{8,0},{12,4},{1,9},{5,13},{9,1},{13,5},{2,10},{6,14},... | collective-permute-start | bytes 1966088 | tf_op jit(solution)/shard_map/ppermute | solution.py:24
  87.5 18.8 %collective-permute-start.2 = (bf16[160,2048]{1,0:T(8,128)(2,1)}, bf16[160,2048]{1,0:T(8,128)(2,1)S(1)}, u32[]{:S(2)}, u32[]{:S(2)}) collective-permute-start(bf16[160,2048]{1,0:T(8,128)(2,1)} %collective-permute-done.1), channel_id=1, source_target_pairs={{0,16},{16,0},{1,17},{17,1},{2,18},{18,2},{3,19},{19,3},{4,20},{20... | collective-permute-start | bytes 1966088 | tf_op jit(solution)/shard_map/ppermute | solution.py:25
  102.9 7.8 %collective-permute-start.3 = (bf16[160,2048]{1,0:T(8,128)(2,1)}, bf16[160,2048]{1,0:T(8,128)(2,1)S(1)}, u32[]{:S(2)}, u32[]{:S(2)}) collective-permute-start(bf16[160,2048]{1,0:T(8,128)(2,1)} %collective-permute-done.1), channel_id=1, source_target_pairs={{0,4},{4,0},{8,12},{12,8},{1,5},{5,1},{9,13},{13,9},{2,6},{6,2},{1... | collective-permute-start | bytes 1966088 | tf_op jit(solution)/shard_map/ppermute | solution.py:28
  110.4 24.6 %collective-permute-start.17 = (bf16[256,2048]{1,0:T(8,128)(2,1)}, bf16[256,2048]{1,0:T(8,128)(2,1)}, u32[]{:S(2)}, u32[]{:S(2)}) collective-permute-start(bf16[256,2048]{1,0:T(8,128)(2,1)} %get-tuple-element.16), channel_id=1, source_target_pairs={{0,8},{4,12},{8,0},{12,4},{1,9},{5,13},{9,1},{13,5},{2,10},{6,14},... | collective-permute-start | bytes 3145736 | tf_op jit(solution)/shard_map/ppermute | solution.py:24
  110.7 31.9 %collective-permute-start.8 = (bf16[512,1024]{1,0:T(8,128)(2,1)}, bf16[512,1024]{1,0:T(8,128)(2,1)S(1)}, u32[]{:S(2)}, u32[]{:S(2)}) collective-permute-start(bf16[512,1024]{1,0:T(8,128)(2,1)} %collective-permute-done.6), channel_id=1, source_target_pairs={{0,4},{4,0},{8,12},{12,8},{1,5},{5,1},{9,13},{13,9},{2,6},{6,2},{1... | collective-permute-start | bytes 3145736 | tf_op jit(solution)/shard_map/ppermute | solution.py:28
  112.3 30.7 %collective-permute-start.7 = (bf16[512,1024]{1,0:T(8,128)(2,1)}, bf16[512,1024]{1,0:T(8,128)(2,1)S(1)}, u32[]{:S(2)}, u32[]{:S(2)}) collective-permute-start(bf16[512,1024]{1,0:T(8,128)(2,1)} %collective-permute-done.6), channel_id=1, source_target_pairs={{0,16},{16,0},{1,17},{17,1},{2,18},{18,2},{3,19},{19,3},{4,20},{20... | collective-permute-start | bytes 3145736 | tf_op jit(solution)/shard_map/ppermute | solution.py:25
  125.9 31.6 %collective-permute-start.15 = (bf16[256,2048]{1,0:T(8,128)(2,1)S(1)}, bf16[256,2048]{1,0:T(8,128)(2,1)}, u32[]{:S(2)}, u32[]{:S(2)}) collective-permute-start(bf16[256,2048]{1,0:T(8,128)(2,1)S(1)} %copy-done.2), channel_id=1, source_target_pairs={{0,8},{4,12},{8,0},{12,4},{1,9},{5,13},{9,1},{13,5},{2,10},{6,14},... | collective-permute-start | bytes 3145736 | tf_op jit(solution)/shard_map/ppermute | solution.py:24
  135.0 22.7 %collective-permute-start.12 = (bf16[512,1024]{1,0:T(8,128)(2,1)}, bf16[512,1024]{1,0:T(8,128)(2,1)S(1)}, u32[]{:S(2)}, u32[]{:S(2)}) collective-permute-start(bf16[512,1024]{1,0:T(8,128)(2,1)} %collective-permute-done.10), channel_id=1, source_target_pairs={{0,4},{4,0},{8,12},{12,8},{1,5},{5,1},{9,13},{13,9},{2,6},{6,2},{1... | collective-permute-start | bytes 3145736 | tf_op jit(solution)/shard_map/ppermute | solution.py:28
  137.2 25.0 %collective-permute-start.11 = (bf16[512,1024]{1,0:T(8,128)(2,1)}, bf16[512,1024]{1,0:T(8,128)(2,1)S(1)}, u32[]{:S(2)}, u32[]{:S(2)}) collective-permute-start(bf16[512,1024]{1,0:T(8,128)(2,1)} %collective-permute-done.10), channel_id=1, source_target_pairs={{0,16},{16,0},{1,17},{17,1},{2,18},{18,2},{3,19},{19,3},{4,20},{20... | collective-permute-start | bytes 3145736 | tf_op jit(solution)/shard_map/ppermute | solution.py:25
  142.6 85.1 %collective-permute-start.14 = (bf16[1024,2048]{1,0:T(8,128)(2,1)}, bf16[1024,2048]{1,0:T(8,128)(2,1)}, u32[]{:S(2)}, u32[]{:S(2)}) collective-permute-start(bf16[1024,2048]{1,0:T(8,128)(2,1)} %param.15), channel_id=1, source_target_pairs={{0,4},{4,0},{8,12},{12,8},{1,5},{5,1},{9,13},{13,9},{2,6},{6,2},{1... | collective-permute-start | bytes 12582920 | tf_op jit(solution)/shard_map/ppermute | solution.py:19
  143.0 21.3 %collective-permute-start.9 = (bf16[512,1024]{1,0:T(8,128)(2,1)S(1)}, bf16[512,1024]{1,0:T(8,128)(2,1)S(1)}, u32[]{:S(2)}, u32[]{:S(2)}) collective-permute-start(bf16[512,1024]{1,0:T(8,128)(2,1)S(1)} %collective-permute-done.7), channel_id=1, source_target_pairs={{0,4},{4,0},{8,12},{12,8},{1,5},{5,1},{9,13},{13,9},{2,6},{6,2},{1... | collective-permute-start | bytes 3145736 | tf_op jit(solution)/shard_map/ppermute | solution.py:29
  157.5 27.3 %collective-permute-start.16 = (bf16[256,2048]{1,0:T(8,128)(2,1)}, bf16[256,2048]{1,0:T(8,128)(2,1)}, u32[]{:S(2)}, u32[]{:S(2)}) collective-permute-start(bf16[256,2048]{1,0:T(8,128)(2,1)} %collective-permute-done.15), channel_id=1, source_target_pairs={{0,16},{16,0},{1,17},{17,1},{2,18},{18,2},{3,19},{19,3},{4,20},{20... | collective-permute-start | bytes 3145736 | tf_op jit(solution)/shard_map/ppermute | solution.py:25
  157.7 49.4 %collective-permute-start.18 = (bf16[256,2048]{1,0:T(8,128)(2,1)}, bf16[256,2048]{1,0:T(8,128)(2,1)S(1)}, u32[]{:S(2)}, u32[]{:S(2)}) collective-permute-start(bf16[256,2048]{1,0:T(8,128)(2,1)} %collective-permute-done.17), channel_id=1, source_target_pairs={{0,16},{16,0},{1,17},{17,1},{2,18},{18,2},{3,19},{19,3},{4,20},{20... | collective-permute-start | bytes 3145736 | tf_op jit(solution)/shard_map/ppermute | solution.py:25
  162.2 45.7 %collective-permute-start.13 = (bf16[512,1024]{1,0:T(8,128)(2,1)S(1)}, bf16[512,1024]{1,0:T(8,128)(2,1)S(1)}, u32[]{:S(2)}, u32[]{:S(2)}) collective-permute-start(bf16[512,1024]{1,0:T(8,128)(2,1)S(1)} %collective-permute-done.11), channel_id=1, source_target_pairs={{0,4},{4,0},{8,12},{12,8},{1,5},{5,1},{9,13},{13,9},{2,6},{6,2},{1... | collective-permute-start | bytes 3145736 | tf_op jit(solution)/shard_map/ppermute | solution.py:29
  164.3 67.9 %collective-permute-start.21 = (bf16[256,2048]{1,0:T(8,128)(2,1)}, bf16[256,2048]{1,0:T(8,128)(2,1)S(1)}, u32[]{:S(2)}, u32[]{:S(2)}) collective-permute-start(bf16[256,2048]{1,0:T(8,128)(2,1)} %collective-permute-done.17), channel_id=1, source_target_pairs={{0,4},{4,0},{8,12},{12,8},{1,5},{5,1},{9,13},{13,9},{2,6},{6,2},{1... | collective-permute-start | bytes 3145736 | tf_op jit(solution)/shard_map/ppermute | solution.py:28
  184.7 47.9 %collective-permute-start.19 = (bf16[256,2048]{1,0:T(8,128)(2,1)}, bf16[256,2048]{1,0:T(8,128)(2,1)}, u32[]{:S(2)}, u32[]{:S(2)}) collective-permute-start(bf16[256,2048]{1,0:T(8,128)(2,1)} %collective-permute-done.15), channel_id=1, source_target_pairs={{0,4},{4,0},{8,12},{12,8},{1,5},{5,1},{9,13},{13,9},{2,6},{6,2},{1... | collective-permute-start | bytes 3145736 | tf_op jit(solution)/shard_map/ppermute | solution.py:28
  207.1 28.7 %collective-permute-start.20 = (bf16[256,2048]{1,0:T(8,128)(2,1)}, bf16[256,2048]{1,0:T(8,128)(2,1)}, u32[]{:S(2)}, u32[]{:S(2)}) collective-permute-start(bf16[256,2048]{1,0:T(8,128)(2,1)} %collective-permute-done.16), channel_id=1, source_target_pairs={{0,4},{4,0},{8,12},{12,8},{1,5},{5,1},{9,13},{13,9},{2,6},{6,2},{1... | collective-permute-start | bytes 3145736 | tf_op jit(solution)/shard_map/ppermute | solution.py:29
  207.9 29.7 %collective-permute-start.22 = (bf16[256,2048]{1,0:T(8,128)(2,1)S(1)}, bf16[256,2048]{1,0:T(8,128)(2,1)S(1)}, u32[]{:S(2)}, u32[]{:S(2)}) collective-permute-start(bf16[256,2048]{1,0:T(8,128)(2,1)S(1)} %collective-permute-done.18), channel_id=1, source_target_pairs={{0,4},{4,0},{8,12},{12,8},{1,5},{5,1},{9,13},{13,9},{2,6},{6,2},{1... | collective-permute-start | bytes 3145736 | tf_op jit(solution)/shard_map/ppermute | solution.py:29
  (12 other events, 139.4 us)
Sparse Core Ops, SparseCore 0:
  8.9 81.9 all-gather.2
  239.3 76.6 reduce-scatter.1

commit v2 on v0

--- a/solution.py
+++ b/solution.py
@@ -1,6 +1,10 @@
+import functools
+
 import jax
 import jax.numpy as jnp
 from jax import lax
+from jax.experimental import pallas as pl
+from jax.experimental.pallas import tpu as pltpu
 from jax.sharding import PartitionSpec as P
 
 HEAD_DIM = 128
@@ -30,7 +34,7 @@
     )
 
 
-def body(tokens, gain, w_query, w_key, w_value, w_out, latents, image_pos, doc_lengths, alpha):
+def plain_body(tokens, gain, w_query, w_key, w_value, w_out, latents, image_pos, doc_lengths, alpha):
     tok_rows = tokens.shape[0]
     gathered, full_gain = (
         lax.all_gather(tokens, "shard", axis=1, tiled=True),
@@ -102,6 +106,494 @@
     return (tokens.astype(jnp.float32) + factor[:, None] * branch).astype(jnp.bfloat16)
 
 
+MESH_ID = pl.DeviceIdType.MESH
+F32, BF16 = jnp.float32, jnp.bfloat16
+
+CARRY = 0
+TOK_UP, TOK_DOWN = 3, 6
+KV = 9
+QUERY = 14
+OUT = 23
+SUM_UP, SUM_DOWN = 32, 36
+TRANSFERS = 40
+CHUNKS = 2
+
+
+def kernel(
+    slots,
+    lat_rows,
+    pos_ref,
+    docs_ref,
+    gate_ref,
+    tok_in,
+    tok_ref,
+    wq_in,
+    wkv_in,
+    wout_in,
+    carry_in,
+    lat_ref,
+    out_ref,
+    tok,
+    wq,
+    wkv,
+    wout,
+    carry,
+    lat_all,
+    kv,
+    qacc,
+    att,
+    part,
+    up_buf,
+    down_buf,
+    send_sem,
+    recv_sem,
+    own_sem,
+):
+    group, mine, z = lax.axis_index("groups"), lax.axis_index("ctx"), lax.axis_index("shard")
+    rows_t = tok_ref.shape[0]
+    x, core = mine // 2, mine % 2
+    near = x * 2 + 1 - core
+    far = (1 - x) * 2 + core
+    diagonal = (1 - x) * 2 + 1 - core
+
+    def at(ctx=None, groups=None, shard=None):
+        return (
+            group if groups is None else groups,
+            mine if ctx is None else ctx,
+            z if shard is None else shard,
+        )
+
+    def copy(number, src, dst, device):
+        return pltpu.make_async_remote_copy(
+            src_ref=src,
+            dst_ref=dst,
+            send_sem=send_sem.at[number],
+            recv_sem=recv_sem.at[number],
+            device_id=device,
+            device_id_type=MESH_ID,
+        )
+
+    barrier = pltpu.get_barrier_semaphore()
+    for device in (at(ctx=near), at(ctx=far), at(ctx=diagonal), at(groups=1 - group)):
+        pl.semaphore_signal(barrier, inc=1, device_id=device, device_id_type=MESH_ID)
+
+    @pl.when(z > 0)
+    def _():
+        pl.semaphore_signal(barrier, inc=1, device_id=at(shard=z - 1), device_id_type=MESH_ID)
+
+    @pl.when(z < 3)
+    def _():
+        pl.semaphore_signal(barrier, inc=1, device_id=at(shard=z + 1), device_id_type=MESH_ID)
+
+    @pl.when((z > 0) & (z < 3))
+    def _():
+        pl.semaphore_wait(barrier, 6)
+
+    @pl.when((z == 0) | (z == 3))
+    def _():
+        pl.semaphore_wait(barrier, 5)
+
+    def tok_up(step):
+        src = tok_in if step == 0 else tok.at[z - step]
+        return copy(TOK_UP + step, src, tok.at[z - step], at(shard=z + 1))
+
+    def tok_up_arrival(step):
+        return copy(TOK_UP + step, tok.at[z - 1 - step], tok.at[z - 1 - step], at(shard=z + 1))
+
+    def tok_down(step):
+        src = tok_in if step == 0 else tok.at[z + step]
+        return copy(TOK_DOWN + step, src, tok.at[z + step], at(shard=z - 1))
+
+    def tok_down_arrival(step):
+        return copy(TOK_DOWN + step, tok.at[z + 1 + step], tok.at[z + 1 + step], at(shard=z - 1))
+
+    def start_tokens(step):
+        @pl.when((z - step >= 0) & (z < 3))
+        def _():
+            tok_up(step).start()
+
+        @pl.when((z + step <= 3) & (z > 0))
+        def _():
+            tok_down(step).start()
+
+    def arrived_tokens(step):
+        @pl.when(z - 1 - step >= 0)
+        def _():
+            tok_up_arrival(step).wait_recv()
+
+        @pl.when(z + 1 + step <= 3)
+        def _():
+            tok_down_arrival(step).wait_recv()
+
+    def sent_tokens(step):
+        @pl.when((z - step >= 0) & (z < 3))
+        def _():
+            tok_up(step).wait_send()
+
+        @pl.when((z + step <= 3) & (z > 0))
+        def _():
+            tok_down(step).wait_send()
+
+    class Panels:
+        def __init__(self, number, source, buffer, chunks):
+            self.number, self.source, self.buffer = number, source, buffer
+            self.rows = source.shape[0]
+            self.half = self.rows // 2
+            self.size = self.half // chunks
+            self.chunks = chunks
+
+        def piece(self, owner, first, size):
+            return self.buffer.at[owner, pl.ds(first, size)]
+
+        def first(self, which, chunk):
+            return which * self.half + chunk * self.size
+
+        def near(self):
+            return copy(self.number, self.source, self.buffer.at[mine], at(ctx=near))
+
+        def far(self, chunk):
+            first = self.first(group, chunk)
+            src = self.source.at[pl.ds(first, self.size)]
+            dst = self.piece(mine, first, self.size)
+            return copy(self.number + 1 + 4 * chunk, src, dst, at(ctx=far))
+
+        def handed(self, chunk):
+            ref = self.piece(far, self.first(group, chunk), self.size)
+            return copy(self.number + 2 + 4 * chunk, ref, ref, at(groups=1 - group))
+
+        def diagonal_far(self, chunk):
+            ref = self.piece(far, self.first(group, chunk), self.size)
+            return copy(self.number + 3 + 4 * chunk, ref, ref, at(ctx=near))
+
+        def diagonal_handed(self, chunk):
+            ref = self.piece(far, self.first(1 - group, chunk), self.size)
+            return copy(self.number + 4 + 4 * chunk, ref, ref, at(ctx=near))
+
+        def got_near(self):
+            ref = self.buffer.at[near]
+            copy(self.number, ref, ref, at(ctx=near)).wait_recv()
+
+        def got_far(self, chunk):
+            ref = self.piece(far, self.first(group, chunk), self.size)
+            copy(self.number + 1 + 4 * chunk, ref, ref, at(ctx=far)).wait_recv()
+            self.handed(chunk).start()
+            self.diagonal_far(chunk).start()
+
+        def got_handed(self, chunk):
+            ref = self.piece(far, self.first(1 - group, chunk), self.size)
+            copy(self.number + 2 + 4 * chunk, ref, ref, at(groups=1 - group)).wait_recv()
+            self.diagonal_handed(chunk).start()
+
+        def got_diagonal_far(self, chunk):
+            ref = self.piece(diagonal, self.first(group, chunk), self.size)
+            copy(self.number + 3 + 4 * chunk, ref, ref, at(ctx=near)).wait_recv()
+
+        def got_diagonal_handed(self, chunk):
+            ref = self.piece(diagonal, self.first(1 - group, chunk), self.size)
+            copy(self.number + 4 + 4 * chunk, ref, ref, at(ctx=near)).wait_recv()
+
+        def sent(self):
+            self.near().wait_send()
+            for chunk in range(self.chunks):
+                self.far(chunk).wait_send()
+                self.handed(chunk).wait_send()
+                self.diagonal_far(chunk).wait_send()
+                self.diagonal_handed(chunk).wait_send()
+
+    kv_panels = Panels(KV, wkv_in, wkv, 1)
+    q_panels = Panels(QUERY, wq_in, wq, CHUNKS)
+    out_panels = Panels(OUT, wout_in, wout, CHUNKS)
+
+    carries = [
+        copy(CARRY + i, carry_in, carry.at[mine], at(ctx=peer))
+        for i, peer in enumerate((near, far, diagonal))
+    ]
+    start_tokens(0)
+    for sending in carries:
+        sending.start()
+    kv_panels.far(0).start()
+    kv_panels.near().start()
+    for chunk in range(CHUNKS):
+        q_panels.far(chunk).start()
+    q_panels.near().start()
+    own = [
+        pltpu.make_async_copy(wkv_in, wkv.at[mine], own_sem.at[0]),
+        pltpu.make_async_copy(carry_in, carry.at[mine], own_sem.at[1]),
+        pltpu.make_async_copy(tok_in, tok.at[z], own_sem.at[2]),
+        pltpu.make_async_copy(wq_in, wq.at[mine], own_sem.at[3]),
+        pltpu.make_async_copy(wout_in, wout.at[mine], own_sem.at[4]),
+    ]
+    for local in own:
+        local.start()
+
+    own[1].wait()
+    for i, peer in enumerate((near, far, diagonal)):
+        copy(CARRY + i, carry.at[peer], carry.at[peer], at(ctx=peer)).wait_recv()
+    held_pos = jnp.full((1, 1), -1.0, F32)
+    lat_all[pl.ds(0, lat_rows)] = jnp.zeros((lat_rows, lat_ref.shape[1]), BF16)
+    for block in range(4):
+        tag = carry[block, pl.ds(lat_rows, 16)].astype(F32)
+        place = tag[0:1, 0:1] * 64.0 + tag[0:1, 1:2]
+        newer = (place >= 0.0) & (block < mine)
+        held_pos = jnp.where(newer, place, held_pos)
+        lat_all[pl.ds(0, lat_rows)] = jnp.where(
+            newer, carry[block, pl.ds(0, lat_rows)].astype(F32), lat_all[pl.ds(0, lat_rows)].astype(F32)
+        ).astype(BF16)
+    lat_all[pl.ds(lat_rows, slots * lat_rows)] = lat_ref[...]
+
+    kv_panels.got_far(0)
+    arrived_tokens(0)
+    start_tokens(1)
+    kv_panels.got_handed(0)
+    q_panels.got_far(0)
+    out_panels.near().start()
+    arrived_tokens(1)
+    start_tokens(2)
+
+    own[0].wait()
+    kv_panels.got_near()
+    kv_panels.got_diagonal_far(0)
+    kv_panels.got_diagonal_handed(0)
+    depth = wkv.shape[1]
+    tile = 512
+
+    @pl.loop(0, wkv.shape[2] // tile)
+    def _(step):
+        columns = pl.ds(pl.multiple_of(step * tile, tile), tile)
+        weight = wkv[:, :, columns].reshape(4 * depth, tile)
+        kv[:, columns] = jnp.dot(lat_all[...], weight, preferred_element_type=F32).astype(BF16)
+
+    q_panels.got_far(1)
+    for chunk in range(CHUNKS):
+        out_panels.far(chunk).start()
+    q_panels.got_handed(0)
+    arrived_tokens(2)
+    own[2].wait()
+    for step in range(3):
+        sent_tokens(step)
+
+    strip = 32
+
+    @pl.loop(0, rows_t // strip)
+    def _(step):
+        rows = pl.ds(pl.multiple_of(step * strip, strip), strip)
+        square = jnp.zeros((strip, 1), F32)
+        for block in range(4):
+            wide = tok[block, rows].astype(F32)
+            square = square + jnp.sum(wide * wide, axis=1, keepdims=True)
+        scale = lax.rsqrt(square / (4 * tok.shape[2]) + 1e-6)
+        for block in range(4):
+            gain = tok[block, pl.ds(rows_t, 16)][0:1].astype(F32)
+            tok[block, rows] = (tok[block, rows].astype(F32) * scale * gain).astype(BF16)
+
+    half = wq.shape[1] // 2
+    width = qacc.shape[1]
+    qacc[...] = jnp.zeros_like(qacc)
+
+    def add_queries(owner, which):
+        first = pl.multiple_of(which * half, half)
+
+        @pl.loop(0, width // tile)
+        def _(step):
+            columns = pl.ds(pl.multiple_of(step * tile, tile), tile)
+            qacc[:, columns] += jnp.dot(
+                tok[owner, pl.ds(0, rows_t), pl.ds(first, half)],
+                wq[owner, pl.ds(first, half), columns],
+                preferred_element_type=F32,
+            )
+
+    own[3].wait()
+    for which in range(2):
+        add_queries(mine, which)
+    q_panels.got_near()
+    for which in range(2):
+        add_queries(near, which)
+    add_queries(far, group)
+    for chunk in range(CHUNKS):
+        q_panels.got_diagonal_far(chunk)
+    add_queries(diagonal, group)
+    q_panels.got_handed(1)
+    out_panels.got_far(0)
+    add_queries(far, 1 - group)
+    for chunk in range(CHUNKS):
+        q_panels.got_diagonal_handed(chunk)
+    add_queries(diagonal, 1 - group)
+    att[...] = qacc[...].astype(BF16)
+
+    position = mine * rows_t + lax.broadcasted_iota(jnp.int32, (rows_t, 1), 0)
+    placed = position.astype(F32)
+    begun = (held_pos >= 0.0) & (held_pos <= placed)
+    chosen = jnp.where(begun, 0, -1)
+    chosen_pos = jnp.where(begun, held_pos, -1.0)
+    for slot in range(slots):
+        slot_pos = pos_ref[slot]
+        eligible = (slot_pos >= 0) & (position >= slot_pos)
+        chosen = jnp.where(eligible, slot + 1, chosen)
+        chosen_pos = jnp.where(eligible, jnp.maximum(chosen_pos, slot_pos.astype(F32)), chosen_pos)
+    doc_start = jnp.zeros((rows_t, 1), jnp.int32)
+    start = jnp.int32(0)
+    for doc in range(docs_ref.shape[0]):
+        doc_start = jnp.where(position >= start, jnp.maximum(doc_start, start), doc_start)
+        start = start + docs_ref[doc]
+    opened = (chosen >= 0) & (chosen_pos >= doc_start.astype(F32))
+    factor = jnp.where(opened, gate_ref[0], 0.0)
+    keys = (slots + 1) * lat_rows
+    image = lax.broadcasted_iota(jnp.int32, (rows_t, keys), 1) // lat_rows
+    allowed = image == chosen
+
+    @pl.loop(0, width // HEAD_DIM)
+    def _(head):
+        columns = pl.ds(pl.multiple_of(head * HEAD_DIM, HEAD_DIM), HEAD_DIM)
+        shifted = pl.ds(pl.multiple_of(width + head * HEAD_DIM, HEAD_DIM), HEAD_DIM)
+        scores = lax.dot_general(
+            att[:, columns], kv[:, columns], (((1,), (1,)), ((), ())), preferred_element_type=F32
+        )
+        scores = jnp.where(allowed, scores * (1.0 / HEAD_DIM**0.5), -1e30)
+        grown = jnp.exp(scores - jnp.max(scores, axis=1, keepdims=True))
+        probs = (grown / jnp.sum(grown, axis=1, keepdims=True)).astype(BF16)
+        att[:, columns] = jnp.dot(probs, kv[:, shifted], preferred_element_type=F32).astype(BF16)
+
+    def up(block):
+        return copy(SUM_UP + block, part.at[block], up_buf.at[block - 1], at(shard=z + 1))
+
+    def down(block):
+        return copy(SUM_DOWN + block, part.at[block], down_buf.at[block], at(shard=z - 1))
+
+    def project(block):
+        @pl.loop(0, wout.shape[2] // tile)
+        def _(step):
+            columns = pl.ds(pl.multiple_of(step * tile, tile), tile)
+            part[block, :, columns] = jnp.dot(
+                att[...], wout[block, :, columns], preferred_element_type=F32
+            ).astype(BF16)
+
+    def add(block, ref):
+        @pl.loop(0, rows_t // strip)
+        def _(step):
+            rows = pl.ds(pl.multiple_of(step * strip, strip), strip)
+            part[block, rows] = (part[block, rows].astype(F32) + ref[rows].astype(F32)).astype(BF16)
+
+    def pass_on(block, edge):
+        @pl.when((block > z) & ((z == 0) if edge else (z > 0)))
+        def _():
+            if not edge:
+                up(block).wait_recv()
+                add(block, up_buf.at[block - 1])
+            up(block).start()
+
+        @pl.when((block < z) & ((z == 3) if edge else (z < 3)))
+        def _():
+            if not edge:
+                down(block).wait_recv()
+                add(block, down_buf.at[block])
+            down(block).start()
+
+    order = (3 * x, x + 1, 3 - 3 * x, 2 - x)
+    own[4].wait()
+    out_panels.got_near()
+    for block in order[:2]:
+        project(block)
+        pass_on(block, True)
+    out_panels.got_far(1)
+    out_panels.got_handed(0)
+    for block in order[:1]:
+        pass_on(block, False)
+    out_panels.got_handed(1)
+    for chunk in range(CHUNKS):
+        out_panels.got_diagonal_far(chunk)
+        out_panels.got_diagonal_handed(chunk)
+    for block in order[2:]:
+        project(block)
+        pass_on(block, True)
+    for block in order[1:]:
+        pass_on(block, False)
+
+    @pl.when(z > 0)
+    def _():
+        copy(SUM_UP + z, part.at[z], up_buf.at[z - 1], at(shard=z - 1)).wait_recv()
+        add(z, up_buf.at[z - 1])
+
+    @pl.when(z < 3)
+    def _():
+        copy(SUM_DOWN + z, part.at[z], down_buf.at[z], at(shard=z + 1)).wait_recv()
+        add(z, down_buf.at[z])
+
+    out_ref[...] = (tok_ref[...].astype(F32) + factor * part[z].astype(F32)).astype(BF16)
+
+    for sending in carries:
+        sending.wait_send()
+    for panels in (kv_panels, q_panels, out_panels):
+        panels.sent()
+    for block in range(4):
+
+        @pl.when(block > z)
+        def _():
+            up(block).wait_send()
+
+        @pl.when(block < z)
+        def _():
+            down(block).wait_send()
+
+
+def body(tokens, gain, w_query, w_key, w_value, w_out, latents, image_pos, doc_lengths, alpha):
+    rows_t, features = tokens.shape
+    slots = image_pos.shape[0]
+    lat_rows = latents.shape[0] // slots
+    heads_width, lat_width = w_query.shape[1], latents.shape[1]
+    gain_rows = jnp.broadcast_to(gain[None, :], (16, features))
+    tok_in = jnp.concatenate([tokens, gain_rows], axis=0)
+    wkv = jnp.concatenate([w_key, w_value], axis=1)
+    used = image_pos >= 0
+    last_slot = jnp.maximum(jnp.max(jnp.where(used, jnp.arange(slots, dtype=jnp.int32), -1)), 0)
+    last_pos = jnp.max(jnp.where(used, image_pos, -1))
+    last_rows = lax.dynamic_slice_in_dim(latents, last_slot * lat_rows, lat_rows, 0)
+    column = jnp.arange(lat_width, dtype=jnp.int32)[None, :]
+    digits = jnp.where(column == 0, last_pos // 64, jnp.where(column == 1, last_pos % 64, 0))
+    tag = jnp.broadcast_to(digits, (16, lat_width)).astype(BF16)
+    carry_in = jnp.concatenate([last_rows, tag], axis=0)
+    smem = pl.BlockSpec(memory_space=pltpu.SMEM)
+    vmem = pl.BlockSpec(memory_space=pltpu.VMEM)
+    anywhere = pl.BlockSpec(memory_space=pl.ANY)
+    keys = (slots + 1) * lat_rows
+    return pl.pallas_call(
+        functools.partial(kernel, slots, lat_rows),
+        out_shape=jax.ShapeDtypeStruct(tokens.shape, BF16),
+        in_specs=[smem] * 3 + [anywhere, vmem] + [anywhere] * 4 + [vmem],
+        out_specs=vmem,
+        scratch_shapes=[
+            pltpu.VMEM((4, rows_t + 16, features), BF16),
+            pltpu.VMEM((4,) + w_query.shape, BF16),
+            pltpu.VMEM((4,) + wkv.shape, BF16),
+            pltpu.VMEM((4,) + w_out.shape, BF16),
+            pltpu.VMEM((4,) + carry_in.shape, BF16),
+            pltpu.VMEM((keys, lat_width), BF16),
+            pltpu.VMEM((keys, 2 * heads_width), BF16),
+            pltpu.VMEM((rows_t, heads_width), F32),
+            pltpu.VMEM((rows_t, heads_width), BF16),
+            pltpu.VMEM((4, rows_t, features), BF16),
+            pltpu.VMEM((3, rows_t, features), BF16),
+            pltpu.VMEM((3, rows_t, features), BF16),
+            pltpu.SemaphoreType.DMA((TRANSFERS,)),
+            pltpu.SemaphoreType.DMA((TRANSFERS,)),
+            pltpu.SemaphoreType.DMA((5,)),
+        ],
+        compiler_params=pltpu.CompilerParams(
+            collective_id=0, has_side_effects=True, vmem_limit_bytes=62 * 2**20
+        ),
+    )(
+        image_pos,
+        doc_lengths,
+        jnp.tanh(alpha),
+        tok_in,
+        tokens,
+        w_query,
+        wkv,
+        w_out,
+        carry_in,
+        latents,
+    )
+
+
 def solution(mesh):
     in_specs = (
         P(("groups", "ctx"), "shard"),
@@ -116,4 +608,6 @@
         P(),
     )
     out_specs = P(("groups", "ctx"), "shard")
-    return jax.shard_map(body, mesh=mesh, in_specs=in_specs, out_specs=out_specs, check_vma=False)
+    sizes = (mesh.shape["groups"], mesh.shape["ctx"], mesh.shape["shard"])
+    chosen_body = body if sizes == (2, 4, 4) else plain_body
+    return jax.shard_map(chosen_body, mesh=mesh, in_specs=in_specs, out_specs=out_specs, check_vma=False)

time: 459 us -> 235 us (0.51)
  waiting for transfers between devices: 363 us -> 0 us
  Pallas kernels: 0 us -> 221 us
  matrix products: 34.1 us -> 0 us
  blocking collectives: 28.7 us -> 0 us
  between operations: 15 us -> 4.27 us
    all_gather x5 -> x0, waiting for transfers between devices: 284 us -> none  [the longest x1 102 us: body(): lax.all_gather(w_query, 'ctx', axis=0, tiled=True)]
    pallas_call x0 -> x1, Pallas kernels: none -> 221 us  [body(): pl.pallas_call(functools.partial(kernel, slots, lat_rows), out_shape=jax....]
    reduce_scatter x1 -> x0, waiting for transfers between devices: 76.1 us -> none  [body(): lax.psum_scatter(partial_terms.astype(jnp.bfloat16), 'shard', scatter_dim...]
    dot_general x5 -> x0, matrix products: 31.6 us -> none  [the longest x1 12 us: body(): jnp.dot(attended, out_panel, preferred_element_type=jnp.float32)]
    all_gather x3 -> x0, blocking collectives: 25.6 us -> none  [the longest x2 15 us: carried_in(): pieces = jax.tree.map(lambda part: lax.all_gather(part, axis), value)]
  transfers between devices with their start and end apart: 6 -> 0, of which waited for: 6 -> 0; matrix products, arithmetic and copies ran while one was open for 7% -> 0% of each run, Pallas kernels for 0% -> 0%
where the time goes in v2:
time: 235 us; the launch traced here: 234 us
  Pallas kernels  221 us (94%)
  other arithmetic  5.6 us (2%)
  between operations  4.27 us (2%)
  local copies, waits for them, and re-layouts  3.94 us (2%)
    pallas_call x1, Pallas kernels, body(): pl.pallas_call(functools.partial(kernel, slots, lat_rows), out_shape=jax....  221 us

profile of v2, /device:TPU:3, one launch (start us, length us, event | category | flops | bytes accessed | tf_op | source)
XLA Modules:
  0.0 234.5 jit_solution(6811352313037433228)
XLA Ops:
  0.0 0.0 copy-start
  0.0 0.0 copy-start.1
  0.8 1.4 fusion
  5.6 0.7 broadcast_in_dim.27
  6.3 0.9 constant_dynamic-slice_fusion
  7.3 0.7 pad_maximum_fusion.2.carry_in
  8.0 2.3 %pad_maximum_fusion.1.tok_in = bf16[272,2048]{1,0:T(8,128)(2,1)} fusion(bf16[16,2048]{1,0:T(8,128)(2,1)S(1)} %broadcast_in_dim.27, bf16[256,2048]{1,0:T(8,128)(2,1)} %tok_ref.1), kind=kLoop, calls=%fused_computation.1 | loop fusion | flops 2228224 | bytes 2228224 | tf_op jit(solution)/shard_map/concatenate | solution.py:544
  10.3 0.0 copy-done
  10.3 0.0 copy-done.1
  10.3 1.2 pad_maximum_fusion.wkv_in
  11.5 220.7 %shard_map.100 = bf16[256,2048]{1,0:T(8,128)(2,1)} custom-call(s32[4]{0:T(128)} %pos_ref.1, s32[6]{0:T(128)} %docs_ref.1, f32[1]{0:T(128)S(6)} %tanh.3.gate_ref, bf16[272,2048]{1,0:T(8,128)(2,1)} %pad_maximum_fusion.1.tok_in, bf16[256,2048]{1,0:T(8,128)(2,1)} %tok_ref.1, bf16[2048,1024]{1,0:T(8,128)(2,1)} %wq_in.1, ...), custom_call_target="tpu_custom_call" | custom-call | tf_op jit(solution)/shard_map/pallas_call | solution.py:558
  232.2 2.3 copy.13
  (2 shorter events, 0.0 us)
Async XLA Ops:
  0.0 10.3 %copy-start = (bf16[320,1024]{1,0:T(8,128)(2,1)S(1)}, bf16[320,1024]{1,0:T(8,128)(2,1)}, u32[]{:S(2)}) copy-start(bf16[320,1024]{1,0:T(8,128)(2,1)} %param.14) | copy-start | bytes 1966084
  0.0 10.3 %copy-start.1 = (bf16[320,1024]{1,0:T(8,128)(2,1)S(1)}, bf16[320,1024]{1,0:T(8,128)(2,1)}, u32[]{:S(2)}) copy-start(bf16[320,1024]{1,0:T(8,128)(2,1)} %param.13) | copy-start | bytes 1966084
